TPU v7x, 512 devices: a whole 4x4x16 slice. The times are simulated.
512 devices in a mesh: dp: 16 (over y, x), expert: 32 (over z, core).
Axes of the slice: x: 4, y: 4, z: 16, core: 2. Of those that a mesh axis runs over, the one named last changes fastest.
Arguments:
- tokens: bfloat16 [65536, 2048], P(('dp', 'expert')), may hold values from -6 to 6
- cotangent: bfloat16 [65536, 2048], P(('dp', 'expert')), may hold values from -12 to 12
- routes: int32 [65536, 2], P(('dp', 'expert')), may hold values from 0 to 31, all different within a row; in each aligned block of 128 rows (0 to 127, 128 to 255, ...) at most 10 rows name the same one
- route_weight: float32 [65536, 2], P(('dp', 'expert')), may hold values from 0.2 to 1
- w_gate: bfloat16 [32, 2048, 768], P('expert', 'dp'), may hold values from -0.125 to 0.125
- w_up: bfloat16 [32, 2048, 768], P('expert', 'dp'), may hold values from -0.125 to 0.125
- w_down: bfloat16 [32, 768, 2048], P('expert', None, 'dp'), may hold values from -0.21875 to 0.21875
Outputs:
- mixed: bfloat16 [65536, 2048], P(('dp', 'expert'))
- grad_tokens: bfloat16 [65536, 2048], P(('dp', 'expert'))
- route_grad: float32 [65536, 2], P(('dp', 'expert'))
- grad_down: float32 [32, 768, 2048], P('expert', None, 'dp')
Inputs may be any that keep to these rules, and one draw needn't show every extreme that they name: `routes`: each row names 2 different experts. Within the rows of one device (aligned blocks of 128 tokens) no expert is named more than 10 times, a bound that some block reaches.
All inputs are finite; a program needn't handle non-finite values.
Results may differ from a plain program's by a relative error of at most 0.015.
Values may be sent and summed in bfloat16 or wider, within the bound.
A program may use at most 64 MiB of HBM per device.

v0:
```python
import jax
import jax.numpy as jnp
from jax import lax
from jax.sharding import PartitionSpec as P


def shards(tokens, cotangent, routes, route_weight, w_gate, w_up, w_down):
    token_rows, model_width = tokens.shape
    top_count = routes.shape[1]
    owners = lax.axis_size("expert")
    local_experts = w_gate.shape[0]
    all_experts = local_experts * owners
    capacity = 5 * token_rows * top_count // (4 * all_experts)
    pair_count = token_rows * top_count
    flat_routes = routes.reshape(pair_count)
    one_hot = (flat_routes[:, None] == jnp.arange(all_experts, dtype=jnp.int32)[None, :]).astype(
        jnp.int32
    )
    earlier = jnp.cumsum(one_hot, axis=0) - one_hot
    slot_index = jnp.sum(earlier * one_hot, axis=1)
    target = flat_routes * capacity + slot_index
    source_pair = (
        jnp.full((all_experts * capacity,), pair_count, jnp.int32)
        .at[target]
        .set(jnp.arange(pair_count, dtype=jnp.int32))
    )
    token_index = source_pair // top_count
    tokens_ext = jnp.concatenate([tokens, jnp.zeros((1, model_width), tokens.dtype)], axis=0)
    cot_ext = jnp.concatenate([cotangent, jnp.zeros((1, model_width), cotangent.dtype)], axis=0)
    weight_ext = jnp.concatenate([route_weight.reshape(-1), jnp.zeros((1,), jnp.float32)], axis=0)
    send_rows = tokens_ext[token_index].reshape(all_experts, capacity, model_width)
    send_cot = (
        (weight_ext[source_pair][:, None] * cot_ext[token_index].astype(jnp.float32))
        .astype(jnp.bfloat16)
        .reshape(all_experts, capacity, model_width)
    )
    recv_rows = lax.all_to_all(send_rows, "expert", split_axis=0, concat_axis=1, tiled=True)
    recv_cot = lax.all_to_all(send_cot, "expert", split_axis=0, concat_axis=1, tiled=True)
    full_gate, full_up = (
        lax.all_gather(w_gate, "dp", axis=1, tiled=True),
        lax.all_gather(w_up, "dp", axis=1, tiled=True),
    )
    full_down = lax.all_gather(w_down, "dp", axis=2, tiled=True)
    gate_pre = jnp.einsum("erd,edf->erf", recv_rows, full_gate, preferred_element_type=jnp.float32)
    up_pre = jnp.einsum("erd,edf->erf", recv_rows, full_up, preferred_element_type=jnp.float32)
    sigma = jax.nn.sigmoid(gate_pre)
    activated = gate_pre * sigma
    hidden = (activated * up_pre).astype(jnp.bfloat16)
    outputs = jnp.einsum(
        "erf,efd->erd", hidden, full_down, preferred_element_type=jnp.float32
    ).astype(jnp.bfloat16)
    grad_hidden = jnp.einsum(
        "erd,efd->erf", recv_cot, full_down, preferred_element_type=jnp.float32
    )
    back_out = lax.all_to_all(outputs, "expert", split_axis=1, concat_axis=0, tiled=True)
    grad_gate = (grad_hidden * up_pre * sigma * (1.0 + gate_pre * (1.0 - sigma))).astype(
        jnp.bfloat16
    )
    grad_up = (grad_hidden * activated).astype(jnp.bfloat16)
    grad_rows = (
        jnp.einsum("erf,edf->erd", grad_gate, full_gate, preferred_element_type=jnp.float32)
        + jnp.einsum("erf,edf->erd", grad_up, full_up, preferred_element_type=jnp.float32)
    ).astype(jnp.bfloat16)
    grad_term = jnp.einsum("erf,erd->efd", hidden, recv_cot, preferred_element_type=jnp.float32)
    grad_down = lax.psum_scatter(
        grad_term.astype(jnp.bfloat16), "dp", scatter_dimension=2, tiled=True
    ).astype(jnp.float32)
    back_grad = lax.all_to_all(grad_rows, "expert", split_axis=1, concat_axis=0, tiled=True)
    out_pairs = (
        back_out.reshape(all_experts * capacity, model_width)[target]
        .reshape(token_rows, top_count, model_width)
        .astype(jnp.float32)
    )
    grad_pairs = (
        back_grad.reshape(all_experts * capacity, model_width)[target]
        .reshape(token_rows, top_count, model_width)
        .astype(jnp.float32)
    )
    mixed = jnp.sum(route_weight[:, :, None] * out_pairs, axis=1).astype(jnp.bfloat16)
    route_grad = jnp.sum(cotangent.astype(jnp.float32)[:, None, :] * out_pairs, axis=2)
    grad_tokens = jnp.sum(grad_pairs, axis=1).astype(jnp.bfloat16)
    return (mixed, grad_tokens, route_grad, grad_down)


def solution(mesh):
    in_specs = (
        P(("dp", "expert"), None),
        P(("dp", "expert"), None),
        P(("dp", "expert"), None),
        P(("dp", "expert"), None),
        P("expert", "dp", None),
        P("expert", "dp", None),
        P("expert", None, "dp"),
    )
    out_specs = (
        P(("dp", "expert"), None),
        P(("dp", "expert"), None),
        P(("dp", "expert"), None),
        P("expert", None, "dp"),
    )
    return jax.shard_map(shards, mesh=mesh, in_specs=in_specs, out_specs=out_specs, check_vma=False)
```

profile of v0, /device:TPU:1, one launch (start us, length us, event | category | flops | bytes accessed | tf_op | source)
XLA Modules:
  0.0 461.8 jit_solution(11766481718375549135)
XLA Ops:
  7.2 0.7 all-gather.8.cloned.1.call-update
  7.9 0.7 all-gather.4.cloned.1.call-update
  8.6 0.8 copy.29
  9.4 0.1 eq.29
  9.6 0.1 eq.25
  9.7 0.7 broadcast_multiply_fusion
  10.4 0.6 reduce-window.6
  11.0 0.2 slice_reduce_fusion
  11.2 0.1 copy.28
  11.3 0.1 mul.81
  11.6 1.4 scatter_custom_fusion
  13.0 1.1 concatenate.11
  14.1 2.4 gather_fusion.3
  16.6 2.2 reshape.179
  18.9 0.1 reshape.174
  19.0 2.4 gather_fusion.2
  21.6 3.8 multiply_convert_fusion
  25.4 16.7 %all-to-all-start.2 = ((bf16[32,10,2048]{2,1,0:T(8,128)(2,1)}), bf16[32,10,2048]{2,1,0:T(8,128)(2,1)S(1)}, u32[]{:S(2)}, u32[]{:S(2)}) async-start(bf16[32,10,2048]{2,1,0:T(8,128)(2,1)} %multiply_convert_fusion), calls=%async_computation.2 | async-start | bytes 4194304 | tf_op jit(solution)/shard_map/all_to_all | solution.py:38
  42.2 0.7 all-gather.6.cloned.1.call-update
  42.9 1.1 concatenate.9
  44.0 3.0 gather_fusion
  47.0 3.3 reshape.168
  50.3 90.4 %all-to-all-done.2 = bf16[32,10,2048]{2,1,0:T(8,128)(2,1)S(1)} async-done(((bf16[32,10,2048]{2,1,0:T(8,128)(2,1)}), bf16[32,10,2048]{2,1,0:T(8,128)(2,1)S(1)}, u32[]{:S(2)}, u32[]{:S(2)}) %all-to-all-start.2) | async-done | bytes 1310752 | tf_op jit(solution)/shard_map/all_to_all | solution.py:38
  140.7 5.2 %all-to-all-start = ((bf16[32,10,2048]{2,1,0:T(8,128)(2,1)}), bf16[32,10,2048]{2,1,0:T(8,128)(2,1)}, u32[]{:S(2)}, u32[]{:S(2)}) async-start(bf16[32,10,2048]{2,1,0:T(8,128)(2,1)} %reshape.168), calls=%async_computation | async-start | bytes 4194304 | tf_op jit(solution)/shard_map/all_to_all | solution.py:37
  146.0 1.4 reshape.175
  147.4 97.7 %all-to-all-done = bf16[32,10,2048]{2,1,0:T(8,128)(2,1)} async-done(((bf16[32,10,2048]{2,1,0:T(8,128)(2,1)}), bf16[32,10,2048]{2,1,0:T(8,128)(2,1)}, u32[]{:S(2)}, u32[]{:S(2)}) %all-to-all-start) | async-done | bytes 1310752 | tf_op jit(solution)/shard_map/all_to_all | solution.py:37
  245.1 2.8 reshape.169
  248.0 4.1 fusion
  252.1 4.1 fusion.10
  256.1 4.3 multiply_convert_fusion.3
  260.4 1.3 fusion.4
  261.7 0.6 copy-done.4
  262.3 1.4 fusion.25
  263.7 2.0 copy.51
  265.7 0.5 broadcast.114
  266.2 21.9 %reduce.8 = bf16[320,2048]{1,0:T(8,128)(2,1)} reduce(bf16[320,1,2048]{2,1,0:T(2,128)(2,1)S(1)} %bitcast.84, bf16[]{:T(256)} %broadcast.114), dimensions={1}, to_apply=%bitcast.78.reduce_sub_computation | reduce | bytes 2621442
  288.2 3.2 reshape.239
  291.4 7.0 %all-to-all-start.3 = ((bf16[32,2,10240]{2,1,0:T(2,128)(2,1)}), bf16[32,2,10240]{2,1,0:T(2,128)(2,1)}, u32[]{:S(2)}, u32[]{:S(2)}) async-start(bf16[32,2,10240]{2,1,0:T(2,128)(2,1)} %reshape.239), calls=%async_computation.3 | async-start | bytes 2621440 | tf_op jit(solution)/shard_map/all_to_all | solution.py:68
  298.4 3.3 fusion.12
  301.7 11.3 %copy.36 = bf16[1,768,2048]{1,0,2:T(2,128)(2,1)} copy(bf16[1,768,2048]{2,1,0:T(8,128)(2,1)S(1)} %fusion.12) | data formatting | bytes 6291456
  313.0 5.0 %copy.48 = bf16[2048,1,768]{2,0,1:T(8,128)(2,1)} copy(bf16[2048,1,768]{2,1,0:T(2,128)(2,1)} %bitcast.82) | data formatting | bytes 6291456
  318.0 1.9 copy-done.3
  319.9 2.2 fusion.22
  322.1 2.0 copy.52
  324.1 9.4 %reduce.7 = bf16[320,2048]{1,0:T(8,128)(2,1)} reduce(bf16[320,1,2048]{2,1,0:T(2,128)(2,1)S(1)} %bitcast.85, bf16[]{:T(256)} %broadcast.114), dimensions={1}, to_apply=%bitcast.79.reduce_sub_computation | reduce | bytes 2621442
  333.6 3.4 reshape.237
  337.0 28.3 %all-to-all-done.3 = bf16[32,2,10240]{2,1,0:T(2,128)(2,1)} async-done(((bf16[32,2,10240]{2,1,0:T(2,128)(2,1)}), bf16[32,2,10240]{2,1,0:T(2,128)(2,1)}, u32[]{:S(2)}, u32[]{:S(2)}) %all-to-all-start.3) | async-done | bytes 1310752 | tf_op jit(solution)/shard_map/all_to_all | solution.py:68
  365.3 4.8 %all-to-all-start.1 = ((bf16[32,2,10240]{2,1,0:T(2,128)(2,1)}), bf16[32,2,10240]{2,1,0:T(2,128)(2,1)S(1)}, u32[]{:S(2)}, u32[]{:S(2)}) async-start(bf16[32,2,10240]{2,1,0:T(2,128)(2,1)} %reshape.237), calls=%async_computation.1 | async-start | bytes 2621440 | tf_op jit(solution)/shard_map/all_to_all | solution.py:55
  370.1 1.1 convert_element_type.84
  371.2 8.9 %reshape.240 = bf16[320,1,2048]{2,1,0:T(2,128)(2,1)} reshape(bf16[32,2,10240]{2,1,0:T(2,128)(2,1)} %all-to-all-done.3) | data formatting | bytes 2621440
  380.1 2.5 copy.49
  382.6 2.3 gather_fusion.4
  384.9 1.7 reshape.177
  386.7 3.6 reduce_sum.44
  390.3 46.7 %all-to-all-done.1 = bf16[32,2,10240]{2,1,0:T(2,128)(2,1)S(1)} async-done(((bf16[32,2,10240]{2,1,0:T(2,128)(2,1)}), bf16[32,2,10240]{2,1,0:T(2,128)(2,1)S(1)}, u32[]{:S(2)}, u32[]{:S(2)}) %all-to-all-start.1) | async-done | bytes 1310752 | tf_op jit(solution)/shard_map/all_to_all | solution.py:55
  437.0 3.7 reshape.238
  440.7 2.5 copy.50
  443.2 1.4 gather_fusion.1
  444.6 1.3 reshape.178
  446.0 6.0 %multiply_reduce_fusion = (f32[128,2]{1,0:T(8,128)S(1)}, bf16[128,2048]{1,0:T(8,128)(2,1)}) fusion(f32[128,2,2048]{2,1,0:T(2,128)S(1)} %reshape.178, f32[128,2048]{1,0:T(8,128)} %convert_element_type.84, f32[128,2]{1,0:T(8,128)S(1)} %copy.27), kind=kLoop, calls=%fused_computation.27 | loop fusion | flops 1834752 | bytes 3672064 | tf_op jit(solution)/shard_map/reduce_sum | solution.py:80
  451.9 0.6 copy.35
  452.6 1.1 reshape_bitcast_fusion
  453.7 0.4 copy.37
  454.1 0.8 convert_element_type.87
  (35 shorter events, 0.6 us)
Async XLA Ops:
  7.2 240.8 %all-gather.8.cloned.1.call-start = ((), (), s32[]{:S(2)}) async-start(), calls=%async_computation.7 | async-start | bytes 3342336 | tf_op jit(solution)/shard_map/all_gather | solution.py:43
  7.9 244.2 %all-gather.4.cloned.1.call-start = ((), (), s32[]{:S(2)}) async-start(), calls=%async_computation.5 | async-start | bytes 3342336 | tf_op jit(solution)/shard_map/all_gather | solution.py:40
  16.6 2.2 copy-start.2
  25.4 115.4 %all-to-all-start.2 = ((bf16[32,10,2048]{2,1,0:T(8,128)(2,1)}), bf16[32,10,2048]{2,1,0:T(8,128)(2,1)S(1)}, u32[]{:S(2)}, u32[]{:S(2)}) async-start(bf16[32,10,2048]{2,1,0:T(8,128)(2,1)} %multiply_convert_fusion), calls=%async_computation.2 | async-start | bytes 4194304 | tf_op jit(solution)/shard_map/all_to_all | solution.py:38
  42.1 214.0 %all-gather.6.cloned.1.call-start = ((), (), s32[]{:S(2)}) async-start(), calls=%async_computation.6 | async-start | bytes 3342336 | tf_op jit(solution)/shard_map/all_gather | solution.py:41
  140.7 104.4 %all-to-all-start = ((bf16[32,10,2048]{2,1,0:T(8,128)(2,1)}), bf16[32,10,2048]{2,1,0:T(8,128)(2,1)}, u32[]{:S(2)}, u32[]{:S(2)}) async-start(bf16[32,10,2048]{2,1,0:T(8,128)(2,1)} %reshape.168), calls=%async_computation | async-start | bytes 4194304 | tf_op jit(solution)/shard_map/all_to_all | solution.py:37
  147.4 100.6 %copy-start.1 = (bf16[320,2048]{1,0:T(8,128)(2,1)S(1)}, bf16[320,2048]{1,0:T(8,128)(2,1)}, u32[]{:S(2)}) copy-start(bf16[320,2048]{1,0:T(8,128)(2,1)} %reshape.175) | copy-start | bytes 3932164
  256.1 4.3 copy-start.6
  256.1 4.3 copy-start.5
  256.1 4.3 copy-start.7
  260.4 1.9 copy-start.4
  291.4 73.9 %all-to-all-start.3 = ((bf16[32,2,10240]{2,1,0:T(2,128)(2,1)}), bf16[32,2,10240]{2,1,0:T(2,128)(2,1)}, u32[]{:S(2)}, u32[]{:S(2)}) async-start(bf16[32,2,10240]{2,1,0:T(2,128)(2,1)} %reshape.239), calls=%async_computation.3 | async-start | bytes 2621440 | tf_op jit(solution)/shard_map/all_to_all | solution.py:68
  298.3 154.2 %reduce-scatter.4.cloned.1.call-start = ((), (), s32[]{:S(2)}) async-start(), calls=%async_computation.8 | async-start | bytes 3342336
  318.0 1.9 copy-start.3
  333.6 36.5 %copy-start = (bf16[128,2048]{1,0:T(8,128)(2,1)S(1)}, bf16[128,2048]{1,0:T(8,128)(2,1)}, u32[]{:S(2)}) copy-start(bf16[128,2048]{1,0:T(8,128)(2,1)} %param.8) | copy-start | bytes 1572868
  365.3 71.7 %all-to-all-start.1 = ((bf16[32,2,10240]{2,1,0:T(2,128)(2,1)}), bf16[32,2,10240]{2,1,0:T(2,128)(2,1)S(1)}, u32[]{:S(2)}, u32[]{:S(2)}) async-start(bf16[32,2,10240]{2,1,0:T(2,128)(2,1)} %reshape.237), calls=%async_computation.1 | async-start | bytes 2621440 | tf_op jit(solution)/shard_map/all_to_all | solution.py:55
Sparse Core Ops, SparseCore 0:
  11.0 72.3 all-gather.7
  86.3 63.3 all-gather.3
  152.7 62.2 all-gather.5
  318.2 90.4 reduce-scatter.3
where the time goes:
time: 468 us; the launch traced here: 462 us
  waiting for transfers between devices  265 us (57%)
  local copies, waits for them, and re-layouts  79.6 us (17%)
  other arithmetic  48.1 us (10%)
  starting transfers between devices  33.9 us (7%)
  matrix products  20.6 us (4%)
  between operations  14.4 us (3%)
    all_to_all x1, waiting for transfers between devices, shards(): lax.all_to_all(send_rows, 'expert', split_axis=0, concat_axis=1, tiled=True)  97.7 us
    all_to_all x1, waiting for transfers between devices, shards(): lax.all_to_all(send_cot, 'expert', split_axis=0, concat_axis=1, tiled=True)  90.4 us
    all_to_all x1, waiting for transfers between devices, shards(): lax.all_to_all(outputs, 'expert', split_axis=1, concat_axis=0, tiled=True)  46.7 us
    unnamed x30, local copies, waits for them, and re-layouts  46.7 us
    unnamed x2, other arithmetic  31.3 us
    all_to_all x1, waiting for transfers between devices, shards(): lax.all_to_all(grad_rows, 'expert', split_axis=1, concat_axis=0, tiled=True)  28.3 us
    all_to_all x1, starting transfers between devices, shards(): lax.all_to_all(send_cot, 'expert', split_axis=0, concat_axis=1, tiled=True)  16.7 us
  transfers between devices with their start and end apart: 8, of which 4 were waited for; matrix products, arithmetic and copies ran while one was open for 24% of the time, Pallas kernels for 0%

commit v1 on v0

v1 whole, which is shorter than its diff:
```python
import functools
import jax
import jax.numpy as jnp
from jax import lax
from jax.experimental import pallas as pl
from jax.experimental.pallas import tpu as pltpu
from jax.sharding import PartitionSpec as P

CAP = 10
BF = jnp.bfloat16
F32 = jnp.float32
PLANE = [(1, 0), (0, 1), (3, 0), (0, 3), (2, 0), (0, 2), (1, 1), (3, 3),
         (1, 3), (3, 1), (2, 1), (1, 2), (2, 3), (3, 2), (2, 2)]


def dot_nn(a, b):
    return lax.dot_general(a, b, (((1,), (0,)), ((), ())), preferred_element_type=F32)


def dot_nt(a, b):
    return lax.dot_general(a, b, (((1,), (1,)), ((), ())), preferred_element_type=F32)


def iota(shape, dim):
    return lax.broadcasted_iota(jnp.int32, shape, dim)


def kernel(routes, rw, x, cot, wg, wu, wd, mixed, gtok, rgrad, gdown,
           W, sx, sc, rx, rc, RX, RC, H, GG, GU, OO, GP, po, pg, ro, rg, UO, UG, GT, GR, S,
           wss, wrs, tss, trs, bss, brs, gss, grs):
    g = lax.axis_index("dp")
    s = lax.axis_index("expert")
    z, c = s // 2, lax.rem(s, 2)
    px, py = lax.rem(g, 4), g // 4
    me_e = s

    def plane(d):
        return lax.rem(py + d[1], 4) * 4 + lax.rem(px + d[0], 4)

    def dz(pos):
        return jnp.where(lax.rem(pos, 2) == 1, (pos + 1) // 2, 16 - pos // 2)

    bar = pltpu.get_barrier_semaphore()

    @pl.loop(1, 32)
    def _(d):
        pl.semaphore_signal(bar, inc=1, device_id=(g, lax.rem(s + d, 32)))

    for d in PLANE:
        pl.semaphore_signal(bar, inc=1, device_id=(plane(d), s))

    eye = (iota((128, 128), 0) == iota((128, 128), 1))
    eyeb = eye.astype(BF)
    W[g, 0:128] = wg[...]
    W[g, 128:256] = wu[...]
    W[g, 256:384] = dot_nt(eyeb, wd[...]).astype(BF)

    pl.semaphore_wait(bar, 31 + 15)

    def w_copy(i, r, n):
        return pltpu.make_async_remote_copy(
            W.at[g, pl.ds(r, n)], W.at[g, pl.ds(r, n)], wss.at[i], wrs.at[i],
            device_id=(plane(PLANE[i]), s))

    @pl.loop(0, 12)
    def _(p):
        for i in range(15):
            w_copy(i, p * 32, 32).start()

    lanes = iota((128, 128), 1)
    r0, r1 = routes[:, 0:1], routes[:, 1:2]
    h0, h1 = (lanes == r0), (lanes == r1)
    named = (h0.astype(F32) + h1.astype(F32)).astype(BF)
    before = (iota((128, 128), 0) > lanes).astype(BF)
    count = dot_nn(before, named)
    t0 = r0.astype(F32) * CAP + jnp.sum(jnp.where(h0, count, 0.0), axis=1, keepdims=True)
    t1 = r1.astype(F32) * CAP + jnp.sum(jnp.where(h1, count, 0.0), axis=1, keepdims=True)
    u0 = jnp.sum(jnp.where(eye, t0, 0.0), axis=0, keepdims=True)
    u1 = jnp.sum(jnp.where(eye, t1, 0.0), axis=0, keepdims=True)
    slots = iota((384, 128), 0).astype(F32)
    P0, P1 = (slots == u0).astype(BF), (slots == u1).astype(BF)

    S[...] = (iota((256, 256), 1) == lax.rem(iota((256, 256), 0), 16) * 16
              + iota((256, 256), 0) // 16).astype(BF)

    def pack(src, dst, lo, n):
        @pl.loop(0, n)
        def _(q):
            r = pl.multiple_of(lo + q * 32, 32)
            a = src[pl.ds(r, 32), :]
            cols = [jnp.concatenate([a[h * 16:h * 16 + 16, k * 128:k * 128 + 128] for k in range(16)], axis=0)
                    for h in range(2)]
            o = dot_nn(S[...], jnp.concatenate(cols, axis=1)).astype(BF)
            dst[pl.ds(r, 16)] = o[:, :128].reshape(16, 16, 128)
            dst[pl.ds(r + 16, 16)] = o[:, 128:].reshape(16, 16, 128)

    def unpack(src, dst, lo, n):
        @pl.loop(0, n)
        def _(q):
            r = pl.multiple_of(lo + q * 32, 32)
            a = src[pl.ds(r, 32)].reshape(512, 128)
            o = dot_nn(S[...], jnp.concatenate([a[:256], a[256:]], axis=1)).astype(BF)
            for h in range(2):
                dst[pl.ds(r + h * 16, 16), :] = jnp.concatenate(
                    [o[k * 16:k * 16 + 16, h * 128:h * 128 + 128] for k in range(16)], axis=1)

    def tok(kind, pos, hc):
        src, dst = ((sx, rx), (sc, rc))[kind]
        e = lax.rem(z + dz(pos), 16) * 2 + hc
        return pltpu.make_async_remote_copy(
            src.at[pl.ds(e * CAP, CAP)], dst.at[pl.ds((2 * pos + c) * CAP, CAP)],
            tss.at[kind, 2 * pos + hc], trs.at[kind, 2 * pos + c], device_id=(g, e))

    def tok_recv(kind, q):
        src, dst = ((sx, rx), (sc, rc))[kind]
        return pltpu.make_async_remote_copy(
            src.at[pl.ds(0, CAP)], dst.at[pl.ds(q * CAP, CAP)],
            tss.at[kind, q], trs.at[kind, q], device_id=(g, s + 1 - 2 * c))

    def send_tokens(kind):
        src, dst = ((sx, rx), (sc, rc))[kind]
        tok(kind, 0, 1 - c).start()

        @pl.loop(1, 16)
        def _(pos):
            tok(kind, pos, 0).start()
            tok(kind, pos, 1).start()
        dst[pl.ds(c * CAP, CAP)] = src[pl.ds(me_e * CAP, CAP)]

    pa = (P0.astype(F32) + P1.astype(F32)).astype(BF)

    @pl.loop(0, 8)
    def _(m):
        k = pl.ds(pl.multiple_of(m * 256, 256), 256)
        UO[:, k] = dot_nn(pa, x[:, k]).astype(BF)
    pack(UO, sx, 0, 10)
    send_tokens(0)

    @pl.loop(0, 8)
    def _(m):
        k = pl.ds(pl.multiple_of(m * 256, 256), 256)
        cf = cot[:, k].astype(F32)
        v0 = (cf * rw[:, 0:1]).astype(BF)
        v1 = (cf * rw[:, 1:2]).astype(BF)
        UG[:, k] = (dot_nn(P0, v0) + dot_nn(P1, v1)).astype(BF)
    pack(UG, sc, 0, 10)
    send_tokens(1)

    for i in range(15):
        w_copy(i, 0, 384).wait_recv()

    def back(kind, pos, cc):
        src, dst = ((po, ro), (pg, rg))[kind]
        t = lax.rem(z + 16 - lax.rem(dz(pos), 16), 16) * 2 + cc
        return pltpu.make_async_remote_copy(
            src.at[pl.ds((2 * pos + cc) * CAP, CAP)], dst.at[pl.ds(me_e * CAP, CAP)],
            bss.at[kind, 2 * pos + cc], brs.at[kind, me_e], device_id=(g, t))

    def back_recv(kind, e):
        src, dst = ((po, ro), (pg, rg))[kind]
        return pltpu.make_async_remote_copy(
            src.at[pl.ds(0, CAP)], dst.at[pl.ds(e * CAP, CAP)],
            bss.at[kind, e], brs.at[kind, e], device_id=(g, s + 1 - 2 * c))

    for half in range(2):
        for kind in range(2):
            if half == 0:
                tok_recv(kind, 1 - c).wait_recv()

            @pl.loop(half * 16 + (2 if half == 0 else 0), half * 16 + 16)
            def _(q):
                tok_recv(kind, q).wait_recv()
        lo = half * 160
        unpack(rx, RX, lo, 5)
        unpack(rc, RC, lo, 5)
        rows = pl.ds(lo, 160)

        @pl.loop(0, 3)
        def _(n):
            k = pl.ds(pl.multiple_of(n * 256, 256), 256)
            xs, cs = RX[rows, :], RC[rows, :]
            gate = dot_nn(xs, W[:, 0:128, k].reshape(2048, 256))
            up = dot_nn(xs, W[:, 128:256, k].reshape(2048, 256))
            gh = dot_nn(cs, W[:, 256:384, k].reshape(2048, 256))
            sig = jax.nn.sigmoid(gate)
            act = gate * sig
            H[rows, k] = (act * up).astype(BF)
            GG[rows, k] = (gh * up * sig * (1.0 + gate * (1.0 - sig))).astype(BF)
            GU[rows, k] = (gh * act).astype(BF)

        @pl.loop(0, 8)
        def _(m):
            k = pl.ds(pl.multiple_of(m * 256, 256), 256)
            j = pl.ds(2 * m, 2)
            OO[rows, k] = dot_nt(H[rows, :], W[j, 256:384, :].reshape(256, 768)).astype(BF)
            GP[rows, k] = (dot_nt(GG[rows, :], W[j, 0:128, :].reshape(256, 768))
                           + dot_nt(GU[rows, :], W[j, 128:256, :].reshape(256, 768))).astype(BF)
        for kind in range(2):
            src, dst, flat = ((po, ro, OO), (pg, rg, GP))[kind]
            pack(flat, src, lo, 5)
            if half == 0:
                back(kind, 0, 1 - c).start()
                dst[pl.ds(me_e * CAP, CAP)] = src[pl.ds(c * CAP, CAP)]

            @pl.loop(half * 8 + (1 if half == 0 else 0), half * 8 + 8)
            def _(pos):
                back(kind, pos, 0).start()
                back(kind, pos, 1).start()

    HT = jnp.transpose(H[...])

    @pl.loop(0, 8)
    def _(m):
        k = pl.ds(pl.multiple_of(m * 256, 256), 256)
        t = dot_nn(HT, RC[:, k]).astype(BF)
        GT[2 * m] = t[:, :128]
        GT[2 * m + 1] = t[:, 128:]

    def g_copy(i, r, n):
        p = plane(PLANE[i])
        return pltpu.make_async_remote_copy(
            GT.at[p, pl.ds(r, n)], GR.at[i, pl.ds(r, n)], gss.at[i], grs.at[i], device_id=(p, s))

    @pl.loop(0, 4)
    def _(p):
        for i in range(15):
            g_copy(i, p * 192, 192).start()

    slots = iota((128, 384), 1).astype(F32)
    Q0, Q1 = (slots == t0).astype(BF), (slots == t1).astype(BF)
    qa = (Q0.astype(F32) + Q1.astype(F32)).astype(BF)
    UO[320:384, :] = jnp.zeros((64, 2048), BF)
    UG[320:384, :] = jnp.zeros((64, 2048), BF)
    for kind in range(2):
        @pl.loop(0, 32)
        def _(e):
            @pl.when(e != me_e)
            def _():
                back_recv(kind, e).wait_recv()
        if kind == 0:
            unpack(ro, UO, 0, 10)

            def body(m, carry):
                a0, a1 = carry
                k = pl.ds(pl.multiple_of(m * 256, 256), 256)
                o0, o1 = dot_nn(Q0, UO[:, k]), dot_nn(Q1, UO[:, k])
                mixed[:, k] = (rw[:, 0:1] * o0 + rw[:, 1:2] * o1).astype(BF)
                cf = cot[:, k].astype(F32)
                return (a0 + jnp.sum(cf * o0, axis=1, keepdims=True),
                        a1 + jnp.sum(cf * o1, axis=1, keepdims=True))
            a0, a1 = lax.fori_loop(0, 8, body, (jnp.zeros((128, 1), F32), jnp.zeros((128, 1), F32)))
            rgrad[:, 0:1] = a0
            rgrad[:, 1:2] = a1
        else:
            unpack(rg, UG, 0, 10)

            @pl.loop(0, 8)
            def _(m):
                k = pl.ds(pl.multiple_of(m * 256, 256), 256)
                gtok[:, k] = dot_nn(qa, UG[:, k]).astype(BF)

    for i in range(15):
        g_copy(i, 0, 768).wait_recv()

    @pl.loop(0, 12)
    def _(b):
        r = pl.ds(pl.multiple_of(b * 64, 64), 64)
        acc = GT[g, r, :].astype(F32)
        for i in range(15):
            acc = acc + GR[i, r, :].astype(F32)
        gdown[r, :] = acc

    for i in range(15):
        w_copy(i, 0, 384).wait_send()
        g_copy(i, 0, 768).wait_send()
    for kind in range(2):
        tok(kind, 0, 1 - c).wait_send()
        back(kind, 0, 1 - c).wait_send()

        @pl.loop(1, 16)
        def _(pos):
            for h in range(2):
                tok(kind, pos, h).wait_send()
                back(kind, pos, h).wait_send()


def shards(tokens, cotangent, routes, route_weight, w_gate, w_up, w_down):
    rows, width = tokens.shape
    ff = w_gate.shape[2]
    part = w_gate.shape[1]
    tile = lambda: pltpu.VMEM((320, 16, 128), BF)
    flat = lambda n, w: pltpu.VMEM((n, w), BF)
    dma = pltpu.SemaphoreType.DMA
    out = pl.pallas_call(
        kernel,
        out_shape=(
            jax.ShapeDtypeStruct((rows, width), BF),
            jax.ShapeDtypeStruct((rows, width), BF),
            jax.ShapeDtypeStruct((rows, 2), F32),
            jax.ShapeDtypeStruct((ff, part), F32),
        ),
        in_specs=[pl.BlockSpec(memory_space=pltpu.VMEM)] * 7,
        out_specs=[pl.BlockSpec(memory_space=pltpu.VMEM)] * 4,
        scratch_shapes=[
            pltpu.VMEM((16, 384, 768), BF),
            tile(), tile(), tile(), tile(),
            flat(320, 2048), flat(320, 2048),
            flat(320, 768), flat(320, 768), flat(320, 768),
            flat(320, 2048), flat(320, 2048),
            tile(), tile(), tile(), tile(),
            flat(384, 2048), flat(384, 2048),
            pltpu.VMEM((16, 768, 128), BF), pltpu.VMEM((15, 768, 128), BF),
            flat(256, 256),
            dma((15,)), dma((15,)), dma((2, 32)), dma((2, 32)),
            dma((2, 32)), dma((2, 32)), dma((15,)), dma((15,)),
        ],
        compiler_params=pltpu.CompilerParams(
            collective_id=0, has_side_effects=True, vmem_limit_bytes=60 * 2**20),
    )(routes, route_weight, tokens, cotangent, w_gate[0], w_up[0], w_down[0])
    mixed, gtok, rgrad, gdown = out
    return (mixed, gtok, rgrad, gdown[None])


def solution(mesh):
    in_specs = (
        P(("dp", "expert"), None),
        P(("dp", "expert"), None),
        P(("dp", "expert"), None),
        P(("dp", "expert"), None),
        P("expert", "dp", None),
        P("expert", "dp", None),
        P("expert", None, "dp"),
    )
    out_specs = (
        P(("dp", "expert"), None),
        P(("dp", "expert"), None),
        P(("dp", "expert"), None),
        P("expert", None, "dp"),
    )
    return jax.shard_map(shards, mesh=mesh, in_specs=in_specs, out_specs=out_specs, check_vma=False)
```

time: 468 us -> 267 us (0.57)
  waiting for transfers between devices: 265 us -> 0 us
  Pallas kernels: 0 us -> 256 us
  local copies, waits for them, and re-layouts: 79.6 us -> 7.5 us
  other arithmetic: 48.1 us -> 0 us
  starting transfers between devices: 33.9 us -> 0 us
  matrix products: 20.6 us -> 0 us
  between operations: 14.4 us -> 0.65 us
    all_to_all x4 -> x0, waiting for transfers between devices: 263 us -> none  [the longest x1 97.7 us: shards(): lax.all_to_all(send_rows, 'expert', split_axis=0, concat_axis=1, tiled=True)]
    pallas_call x0 -> x1, Pallas kernels: none -> 256 us  [shards(): pl.pallas_call(kernel, out_shape=(jax.ShapeDtypeStruct((rows, width), BF)...]
    unnamed x30 -> x14, local copies, waits for them, and re-layouts: 46.7 us -> 7.5 us
    all_to_all x4 -> x0, starting transfers between devices: 33.7 us -> none  [the longest x1 16.7 us: shards(): lax.all_to_all(send_cot, 'expert', split_axis=0, concat_axis=1, tiled=True)]
    unnamed x2 -> x0, other arithmetic: 31.3 us -> none
    dot_general x7 -> x0, matrix products: 20.6 us -> none  [the longest x1 4.29 us: shards(): jnp.einsum('erd,edf->erf', recv_rows, full_up, preferred_element_type=jnp...]
    gather x5 -> x0, local copies, waits for them, and re-layouts: 11.6 us -> none  [the longest x1 3.03 us: shards(): tokens_ext[token_index].reshape(all_experts, capacity, model_width)]
    reduce_sum x3 -> x0, other arithmetic: 9.69 us -> none  [the longest x1 5.96 us: shards(): jnp.sum(cotangent.astype(jnp.float32)[:, None, :] * out_pairs, axis=2)]
  transfers between devices with their start and end apart: 8 -> 0, of which waited for: 4 -> 0; matrix products, arithmetic and copies ran while one was open for 24% -> 0% of each run, Pallas kernels for 0% -> 0%
where the time goes in v1:
time: 267 us; the launch traced here: 264 us
  Pallas kernels  256 us (96%)
  local copies, waits for them, and re-layouts  7.5 us (3%)
    pallas_call x1, Pallas kernels, shards(): pl.pallas_call(kernel, out_shape=(jax.ShapeDtypeStruct((rows, width), BF)...  256 us
    unnamed x14, local copies, waits for them, and re-layouts  7.5 us

profile of v1, /device:TPU:1, one launch (start us, length us, event | category | flops | bytes accessed | tf_op | source)
XLA Modules:
  0.0 264.3 jit_solution(13831055742781870642)
XLA Ops:
  0.6 0.0 copy-start.2
  0.6 0.7 copy-done.2
  1.3 0.0 copy-start.3
  1.3 0.7 copy.11.routes
  2.1 0.0 copy-done.3
  2.1 0.7 copy.12.rw
  2.8 256.2 %shard_map.102 = (bf16[128,2048]{1,0:T(8,128)(2,1)}, bf16[128,2048]{1,0:T(8,128)(2,1)}, f32[128,2]{1,0:T(8,128)}, f32[768,128]{1,0:T(8,128)}) custom-call(s32[128,2]{1,0:T(8,128)} %copy.11.routes, f32[128,2]{1,0:T(8,128)} %copy.12.rw, bf16[128,2048]{1,0:T(8,128)(2,1)} %x.1, bf16[128,2048]{1,0:T(8,128)(2,1)} %cot.1, bf16[128,768]{1,0:T(8,128)(2,1)} %bitcast.5, ...), custom_call_target="tpu_custom_call" | custom-call | tf_op jit(solution)/shard_map/pallas_call | solution.py:294
  259.0 1.5 copy.13
  260.5 0.0 copy-start
  260.5 1.9 copy.17
  262.4 0.0 copy-done
  262.4 0.0 copy-start.1
  262.4 0.8 copy.18
  263.2 0.4 copy-done.1
  263.6 0.7 copy.19
Async XLA Ops:
  0.6 0.7 copy-start.2
  1.3 0.7 copy-start.3
  260.5 1.9 copy-start
  262.4 1.2 copy-start.1

commit v2 on v1

--- a/solution.py
+++ b/solution.py
@@ -26,19 +26,25 @@
 
 
 def kernel(routes, rw, x, cot, wg, wu, wd, mixed, gtok, rgrad, gdown,
-           W, sx, sc, rx, rc, RX, RC, H, GG, GU, OO, GP, po, pg, ro, rg, UO, UG, GT, GR, S,
-           wss, wrs, tss, trs, bss, brs, gss, grs):
+           W, WZ, sx, sc, rx, rc, RX, RC, H, GG, GU, OO, GP, po, pg, ro, rg, UO, UG, GT, GR, RS, S,
+           wss, wrs, zss, zrs, tss, trs, bss, brs, gss, grs, rss, rrs):
     g = lax.axis_index("dp")
     s = lax.axis_index("expert")
     z, c = s // 2, lax.rem(s, 2)
     px, py = lax.rem(g, 4), g // 4
-    me_e = s
+    me_e = jnp.where(c == 0, 2 * z, 2 * g + 1)
+
+    def on_core(n):
+        return pl.when(c == n)
 
     def plane(d):
         return lax.rem(py + d[1], 4) * 4 + lax.rem(px + d[0], 4)
 
     def dz(pos):
-        return jnp.where(lax.rem(pos, 2) == 1, (pos + 1) // 2, 16 - pos // 2)
+        return jnp.where(lax.rem(pos, 2) == 1, (pos + 1) // 2, lax.rem(16 - pos // 2, 16))
+
+    def up_z(t):
+        return lax.rem(z + t + 16, 16)
 
     bar = pltpu.get_barrier_semaphore()
 
@@ -46,26 +52,61 @@
     def _(d):
         pl.semaphore_signal(bar, inc=1, device_id=(g, lax.rem(s + d, 32)))
 
-    for d in PLANE:
-        pl.semaphore_signal(bar, inc=1, device_id=(plane(d), s))
+    @pl.loop(1, 16)
+    def _(d):
+        pl.semaphore_signal(bar, inc=1, device_id=(lax.rem(g + d, 16), 2 * z))
+        pl.semaphore_signal(bar, inc=1, device_id=(lax.rem(g + d, 16), 2 * z + 1))
 
     eye = (iota((128, 128), 0) == iota((128, 128), 1))
-    eyeb = eye.astype(BF)
-    W[g, 0:128] = wg[...]
-    W[g, 128:256] = wu[...]
-    W[g, 256:384] = dot_nt(eyeb, wd[...]).astype(BF)
-
-    pl.semaphore_wait(bar, 31 + 15)
-
-    def w_copy(i, r, n):
-        return pltpu.make_async_remote_copy(
-            W.at[g, pl.ds(r, n)], W.at[g, pl.ds(r, n)], wss.at[i], wrs.at[i],
-            device_id=(plane(PLANE[i]), s))
-
-    @pl.loop(0, 12)
-    def _(p):
-        for i in range(15):
-            w_copy(i, p * 32, 32).start()
+    down_rows = dot_nt(eye.astype(BF), wd[...]).astype(BF)
+
+    @on_core(0)
+    def _():
+        W[g, 0:128] = wg[...]
+        W[g, 128:256] = wu[...]
+        W[g, 256:384] = down_rows
+
+    @on_core(1)
+    def _():
+        WZ[z, 0:128] = wg[...]
+        WZ[z, 128:256] = wu[...]
+        WZ[z, 256:384] = down_rows
+
+    pl.semaphore_wait(bar, 31 + 30)
+
+    def w_copy(core, i, r, n):
+        p = plane(PLANE[i])
+        src = W.at[g, pl.ds(r, n)] if core == 0 else WZ.at[p, pl.ds(r, n)]
+        return pltpu.make_async_remote_copy(
+            src, W.at[g, pl.ds(r, n)], wss.at[i], wrs.at[i], device_id=(p, s))
+
+    def ring(way, t, h):
+        to = up_z(1 - 2 * way)
+        sl = lax.rem(z + 16 + (t if way else -t), 16)
+        r = pl.ds(h * 192, 192)
+        return pltpu.make_async_remote_copy(
+            WZ.at[sl, r], WZ.at[sl, r], zss.at[way, t, h], zrs.at[way, t, h],
+            device_id=(g, 2 * to + 1))
+
+    def relay(t, last):
+        for h in range(2):
+            for way in range(2):
+                ring(way, t - 1, h).wait_recv()
+                if not last or h == way:
+                    ring(way, t, h).start()
+
+    @on_core(0)
+    def _():
+        @pl.loop(0, 12)
+        def _(p):
+            for i in range(15):
+                w_copy(0, i, p * 32, 32).start()
+
+    @on_core(1)
+    def _():
+        for h in range(2):
+            for way in range(2):
+                ring(way, 0, h).start()
 
     lanes = iota((128, 128), 1)
     r0, r1 = routes[:, 0:1], routes[:, 1:2]
@@ -104,12 +145,22 @@
                 dst[pl.ds(r + h * 16, 16), :] = jnp.concatenate(
                     [o[k * 16:k * 16 + 16, h * 128:h * 128 + 128] for k in range(16)], axis=1)
 
+    def chip(pos, sign):
+        dx, dy = lax.rem(pos, 4), pos // 4
+        return lax.rem(py + sign * dy + 4, 4) * 4 + lax.rem(px + sign * dx + 4, 4)
+
     def tok(kind, pos, hc):
         src, dst = ((sx, rx), (sc, rc))[kind]
-        e = lax.rem(z + dz(pos), 16) * 2 + hc
+        if hc == 0:
+            e = lax.rem(z + dz(pos), 16) * 2
+            dev = (g, e)
+        else:
+            j = chip(pos, 1)
+            e = 2 * j + 1
+            dev = (j, 2 * z + 1)
         return pltpu.make_async_remote_copy(
             src.at[pl.ds(e * CAP, CAP)], dst.at[pl.ds((2 * pos + c) * CAP, CAP)],
-            tss.at[kind, 2 * pos + hc], trs.at[kind, 2 * pos + c], device_id=(g, e))
+            tss.at[kind, 2 * pos + hc], trs.at[kind, 2 * pos + c], device_id=dev)
 
     def tok_recv(kind, q):
         src, dst = ((sx, rx), (sc, rc))[kind]
@@ -117,14 +168,18 @@
             src.at[pl.ds(0, CAP)], dst.at[pl.ds(q * CAP, CAP)],
             tss.at[kind, q], trs.at[kind, q], device_id=(g, s + 1 - 2 * c))
 
-    def send_tokens(kind):
+    def send_tokens(kind, hc, first=0):
+        if first == 0:
+            @on_core(1 - hc)
+            def _():
+                tok(kind, 0, hc).start()
+
+        @pl.loop(max(first, 1), 16)
+        def _(pos):
+            tok(kind, pos, hc).start()
+
+    def keep(kind):
         src, dst = ((sx, rx), (sc, rc))[kind]
-        tok(kind, 0, 1 - c).start()
-
-        @pl.loop(1, 16)
-        def _(pos):
-            tok(kind, pos, 0).start()
-            tok(kind, pos, 1).start()
         dst[pl.ds(c * CAP, CAP)] = src[pl.ds(me_e * CAP, CAP)]
 
     pa = (P0.astype(F32) + P1.astype(F32)).astype(BF)
@@ -134,7 +189,16 @@
         k = pl.ds(pl.multiple_of(m * 256, 256), 256)
         UO[:, k] = dot_nn(pa, x[:, k]).astype(BF)
     pack(UO, sx, 0, 10)
-    send_tokens(0)
+    keep(0)
+    send_tokens(0, 1)
+
+    @on_core(0)
+    def _():
+        send_tokens(0, 0)
+
+    @on_core(1)
+    def _():
+        relay(1, False)
 
     @pl.loop(0, 8)
     def _(m):
@@ -144,17 +208,44 @@
         v1 = (cf * rw[:, 1:2]).astype(BF)
         UG[:, k] = (dot_nn(P0, v0) + dot_nn(P1, v1)).astype(BF)
     pack(UG, sc, 0, 10)
-    send_tokens(1)
+    keep(1)
+    send_tokens(1, 1)
+
+    @on_core(0)
+    def _():
+        send_tokens(1, 0)
+
+    @on_core(1)
+    def _():
+        @pl.loop(2, 7)
+        def _(t):
+            relay(t, False)
+        relay(7, True)
+        for way in range(2):
+            ring(way, 7, way).wait_recv()
+        W[g] = WZ[g]
+        for kind in range(2):
+            tok(kind, 0, 0).start()
+
+        @pl.loop(0, 12)
+        def _(p):
+            for i in range(15):
+                w_copy(1, i, p * 32, 32).start()
+            for kind in range(2):
+                tok(kind, p + 1, 0).start()
+        for kind in range(2):
+            send_tokens(kind, 0, 13)
 
     for i in range(15):
-        w_copy(i, 0, 384).wait_recv()
+        w_copy(0, i, 0, 384).wait_recv()
 
     def back(kind, pos, cc):
         src, dst = ((po, ro), (pg, rg))[kind]
-        t = lax.rem(z + 16 - lax.rem(dz(pos), 16), 16) * 2 + cc
+        dev = (jnp.where(c == 0, g, chip(pos, -1)),
+               jnp.where(c == 0, lax.rem(z + 16 - dz(pos), 16), z) * 2 + cc)
         return pltpu.make_async_remote_copy(
             src.at[pl.ds((2 * pos + cc) * CAP, CAP)], dst.at[pl.ds(me_e * CAP, CAP)],
-            bss.at[kind, 2 * pos + cc], brs.at[kind, me_e], device_id=(g, t))
+            bss.at[kind, 2 * pos + cc], brs.at[kind, me_e], device_id=dev)
 
     def back_recv(kind, e):
         src, dst = ((po, ro), (pg, rg))[kind]
@@ -162,7 +253,7 @@
             src.at[pl.ds(0, CAP)], dst.at[pl.ds(e * CAP, CAP)],
             bss.at[kind, e], brs.at[kind, e], device_id=(g, s + 1 - 2 * c))
 
-    for half in range(2):
+    def phase_a(half):
         for kind in range(2):
             if half == 0:
                 tok_recv(kind, 1 - c).wait_recv()
@@ -187,6 +278,10 @@
             H[rows, k] = (act * up).astype(BF)
             GG[rows, k] = (gh * up * sig * (1.0 + gate * (1.0 - sig))).astype(BF)
             GU[rows, k] = (gh * act).astype(BF)
+
+    def phase_b(half):
+        lo = half * 160
+        rows = pl.ds(lo, 160)
 
         @pl.loop(0, 8)
         def _(m):
@@ -207,37 +302,85 @@
                 back(kind, pos, 0).start()
                 back(kind, pos, 1).start()
 
-    HT = jnp.transpose(H[...])
-
-    @pl.loop(0, 8)
-    def _(m):
-        k = pl.ds(pl.multiple_of(m * 256, 256), 256)
-        t = dot_nn(HT, RC[:, k]).astype(BF)
-        GT[2 * m] = t[:, :128]
-        GT[2 * m + 1] = t[:, 128:]
-
     def g_copy(i, r, n):
         p = plane(PLANE[i])
         return pltpu.make_async_remote_copy(
-            GT.at[p, pl.ds(r, n)], GR.at[i, pl.ds(r, n)], gss.at[i], grs.at[i], device_id=(p, s))
-
-    @pl.loop(0, 4)
-    def _(p):
-        for i in range(15):
-            g_copy(i, p * 192, 192).start()
+            GT.at[p, pl.ds(r, n)], GR.at[g, pl.ds(r, n)], gss.at[i], grs.at[g], device_id=(p, s))
+
+    def g_recv(j):
+        return pltpu.make_async_remote_copy(
+            GT.at[j], GR.at[j], gss.at[0], grs.at[j], device_id=(g, s + 1 - 2 * c))
+
+    def gradients():
+        HT = jnp.transpose(H[...])
+
+        @pl.loop(0, 8)
+        def _(m):
+            k = pl.ds(pl.multiple_of(m * 256, 256), 256)
+            t = dot_nn(HT, RC[:, k]).astype(BF)
+            GT[2 * m] = t[:, :128]
+            GT[2 * m + 1] = t[:, 128:]
+
+        @pl.loop(0, 4)
+        def _(p):
+            for i in range(15):
+                g_copy(i, p * 192, 192).start()
+        GR[g] = GT[g]
+
+    def hop(way, t, h, first=False):
+        to = up_z(1 - 2 * way)
+        j = lax.rem(z + 16 + (t - 7 if way else 8 - t), 16)
+        r = pl.ds(h * 384, 384)
+        src = GR.at[j, r] if first else RS.at[way, t - 1, r]
+        return j, pltpu.make_async_remote_copy(
+            src, RS.at[way, t, r], rss.at[way, t, h], rrs.at[way, t, h], device_id=(g, 2 * to + 1))
+
+    def g_wait(j):
+        @pl.when(j != g)
+        def _():
+            g_recv(j).wait_recv()
+
+    def reduce_z():
+        for way in range(2):
+            for h in range(2):
+                j, cp = hop(way, 0, h, True)
+                if h == 0:
+                    g_wait(j)
+                cp.start()
+
+        def step(t, ways):
+            for h in range(2):
+                for way in ways:
+                    j, cp = hop(way, t, h)
+                    if h == 0:
+                        g_wait(j)
+                    hop(way, t - 1, h, True)[1].wait_recv()
+
+                    @pl.loop(0, 6)
+                    def _(b):
+                        r = pl.ds(pl.multiple_of(h * 384 + b * 64, 64), 64)
+                        RS[way, t - 1, r, :] = (RS[way, t - 1, r, :].astype(F32)
+                                                + GR[j, r, :].astype(F32)).astype(BF)
+                    cp.start()
+
+        @pl.loop(1, 7)
+        def _(t):
+            step(t, (0, 1))
+        step(7, (0,))
+        g_wait(z)
 
     slots = iota((128, 384), 1).astype(F32)
     Q0, Q1 = (slots == t0).astype(BF), (slots == t1).astype(BF)
     qa = (Q0.astype(F32) + Q1.astype(F32)).astype(BF)
-    UO[320:384, :] = jnp.zeros((64, 2048), BF)
-    UG[320:384, :] = jnp.zeros((64, 2048), BF)
-    for kind in range(2):
+
+    def combine(kind):
         @pl.loop(0, 32)
         def _(e):
             @pl.when(e != me_e)
             def _():
                 back_recv(kind, e).wait_recv()
         if kind == 0:
+            UO[320:384, :] = jnp.zeros((64, 2048), BF)
             unpack(ro, UO, 0, 10)
 
             def body(m, carry):
@@ -252,6 +395,7 @@
             rgrad[:, 0:1] = a0
             rgrad[:, 1:2] = a1
         else:
+            UG[320:384, :] = jnp.zeros((64, 2048), BF)
             unpack(rg, UG, 0, 10)
 
             @pl.loop(0, 8)
@@ -259,29 +403,85 @@
                 k = pl.ds(pl.multiple_of(m * 256, 256), 256)
                 gtok[:, k] = dot_nn(qa, UG[:, k]).astype(BF)
 
+    @on_core(0)
+    def _():
+        for half in range(2):
+            phase_a(half)
+            phase_b(half)
+        gradients()
+
+    @on_core(1)
+    def _():
+        phase_a(0)
+        phase_a(1)
+        gradients()
+        phase_b(0)
+        phase_b(1)
+        reduce_z()
+
+    combine(0)
+    combine(1)
+
+    @on_core(0)
+    def _():
+        @pl.loop(0, 16)
+        def _(j):
+            g_wait(j)
+
+        @pl.loop(0, 12)
+        def _(b):
+            r = pl.ds(pl.multiple_of(b * 64, 64), 64)
+            acc = GR[0, r, :].astype(F32)
+            for i in range(1, 16):
+                acc = acc + GR[i, r, :].astype(F32)
+            gdown[r, :] = acc
+
+    @on_core(1)
+    def _():
+        for h in range(2):
+            hop(0, 7, h, True)[1].wait_recv()
+            hop(1, 6, h, True)[1].wait_recv()
+
+        @pl.loop(0, 12)
+        def _(b):
+            r = pl.ds(pl.multiple_of(b * 64, 64), 64)
+            gdown[r, :] = (GR[z, r, :].astype(F32) + RS[0, 7, r, :].astype(F32)) + RS[1, 6, r, :].astype(F32)
+
     for i in range(15):
-        g_copy(i, 0, 768).wait_recv()
-
-    @pl.loop(0, 12)
-    def _(b):
-        r = pl.ds(pl.multiple_of(b * 64, 64), 64)
-        acc = GT[g, r, :].astype(F32)
-        for i in range(15):
-            acc = acc + GR[i, r, :].astype(F32)
-        gdown[r, :] = acc
-
-    for i in range(15):
-        w_copy(i, 0, 384).wait_send()
+        w_copy(0, i, 0, 384).wait_send()
         g_copy(i, 0, 768).wait_send()
     for kind in range(2):
-        tok(kind, 0, 1 - c).wait_send()
-        back(kind, 0, 1 - c).wait_send()
+        @on_core(0)
+        def _():
+            tok(kind, 0, 1).wait_send()
+            back(kind, 0, 1).wait_send()
+
+        @on_core(1)
+        def _():
+            tok(kind, 0, 0).wait_send()
+            back(kind, 0, 0).wait_send()
 
         @pl.loop(1, 16)
         def _(pos):
             for h in range(2):
                 tok(kind, pos, h).wait_send()
                 back(kind, pos, h).wait_send()
+
+    @on_core(1)
+    def _():
+        for way in range(2):
+            @pl.loop(0, 7)
+            def _(t):
+                for h in range(2):
+                    ring(way, t, h).wait_send()
+            ring(way, 7, way).wait_send()
+            for h in range(2):
+                hop(way, 0, h, True)[1].wait_send()
+
+            @pl.loop(1, 8 - way)
+            def _(t):
+                for h in range(2):
+                    hop(way, t, h, True)[1].wait_send()
 
 
 def shards(tokens, cotangent, routes, route_weight, w_gate, w_up, w_down):
@@ -302,17 +502,19 @@
         in_specs=[pl.BlockSpec(memory_space=pltpu.VMEM)] * 7,
         out_specs=[pl.BlockSpec(memory_space=pltpu.VMEM)] * 4,
         scratch_shapes=[
-            pltpu.VMEM((16, 384, 768), BF),
+            pltpu.VMEM((16, 384, 768), BF), pltpu.VMEM((16, 384, 768), BF),
             tile(), tile(), tile(), tile(),
             flat(320, 2048), flat(320, 2048),
             flat(320, 768), flat(320, 768), flat(320, 768),
             flat(320, 2048), flat(320, 2048),
             tile(), tile(), tile(), tile(),
             flat(384, 2048), flat(384, 2048),
-            pltpu.VMEM((16, 768, 128), BF), pltpu.VMEM((15, 768, 128), BF),
+            pltpu.VMEM((16, 768, 128), BF), pltpu.VMEM((16, 768, 128), BF),
+            pltpu.VMEM((2, 8, 768, 128), BF),
             flat(256, 256),
-            dma((15,)), dma((15,)), dma((2, 32)), dma((2, 32)),
-            dma((2, 32)), dma((2, 32)), dma((15,)), dma((15,)),
+            dma((15,)), dma((15,)), dma((2, 8, 2)), dma((2, 8, 2)),
+            dma((2, 32)), dma((2, 32)), dma((2, 32)), dma((2, 32)),
+            dma((15,)), dma((16,)), dma((2, 8, 2)), dma((2, 8, 2)),
         ],
         compiler_params=pltpu.CompilerParams(
             collective_id=0, has_side_effects=True, vmem_limit_bytes=60 * 2**20),

time: 267 us -> 236 us (0.88)
  Pallas kernels: 256 us -> 228 us
    pallas_call x1, Pallas kernels: 256 us -> 228 us  [shards(): pl.pallas_call(kernel, out_shape=(jax.ShapeDtypeStruct((rows, width), BF)...]
where the time goes in v2:
time: 236 us
  Pallas kernels  228 us (97%)
  local copies, waits for them, and re-layouts  7.5 us (3%)
    pallas_call x1, Pallas kernels, shards(): pl.pallas_call(kernel, out_shape=(jax.ShapeDtypeStruct((rows, width), BF)...  228 us
    unnamed x14, local copies, waits for them, and re-layouts  7.5 us

profile of v2, /device:TPU:1, one launch (start us, length us, event | category | flops | bytes accessed | tf_op | source)
XLA Modules:
  0.0 235.7 jit_solution(11260590000102509356)
XLA Ops:
  0.6 0.0 copy-start.2
  0.6 0.7 copy-done.2
  1.3 0.0 copy-start.3
  1.3 0.7 copy.11.routes
  2.1 0.0 copy-done.3
  2.1 0.7 copy.12.rw
  2.8 227.6 %shard_map.102 = (bf16[128,2048]{1,0:T(8,128)(2,1)}, bf16[128,2048]{1,0:T(8,128)(2,1)}, f32[128,2]{1,0:T(8,128)}, f32[768,128]{1,0:T(8,128)}) custom-call(s32[128,2]{1,0:T(8,128)} %copy.11.routes, f32[128,2]{1,0:T(8,128)} %copy.12.rw, bf16[128,2048]{1,0:T(8,128)(2,1)} %x.1, bf16[128,2048]{1,0:T(8,128)(2,1)} %cot.1, bf16[128,768]{1,0:T(8,128)(2,1)} %bitcast.5, ...), custom_call_target="tpu_custom_call" | custom-call | tf_op jit(solution)/shard_map/pallas_call | solution.py:494
  230.4 1.5 copy.13
  231.9 0.0 copy-start
  231.9 1.9 copy.17
  233.8 0.0 copy-done
  233.8 0.0 copy-start.1
  233.8 0.8 copy.18
  234.6 0.4 copy-done.1
  235.0 0.7 copy.19
Async XLA Ops:
  0.6 0.7 copy-start.2
  1.3 0.7 copy-start.3
  231.9 1.9 copy-start
  233.8 1.2 copy-start.1

commit v3 on v2

--- a/solution.py
+++ b/solution.py
@@ -27,7 +27,7 @@
 
 def kernel(routes, rw, x, cot, wg, wu, wd, mixed, gtok, rgrad, gdown,
            W, WZ, sx, sc, rx, rc, RX, RC, H, GG, GU, OO, GP, po, pg, ro, rg, UO, UG, GT, GR, RS, S,
-           wss, wrs, zss, zrs, tss, trs, bss, brs, gss, grs, rss, rrs):
+           wss, wrs, zss, zrs, tss, trs, bss, brs, gss, grs, rss, rrs, go):
     g = lax.axis_index("dp")
     s = lax.axis_index("expert")
     z, c = s // 2, lax.rem(s, 2)
@@ -83,16 +83,16 @@
     def ring(way, t, h):
         to = up_z(1 - 2 * way)
         sl = lax.rem(z + 16 + (t if way else -t), 16)
-        r = pl.ds(h * 192, 192)
+        r = pl.ds(h * 64, 64)
         return pltpu.make_async_remote_copy(
             WZ.at[sl, r], WZ.at[sl, r], zss.at[way, t, h], zrs.at[way, t, h],
             device_id=(g, 2 * to + 1))
 
     def relay(t, last):
-        for h in range(2):
+        for h in range(6):
             for way in range(2):
                 ring(way, t - 1, h).wait_recv()
-                if not last or h == way:
+                if not last or h // 3 == way:
                     ring(way, t, h).start()
 
     @on_core(0)
@@ -104,20 +104,28 @@
 
     @on_core(1)
     def _():
-        for h in range(2):
+        for h in range(6):
             for way in range(2):
                 ring(way, 0, h).start()
 
     lanes = iota((128, 128), 1)
-    r0, r1 = routes[:, 0:1], routes[:, 1:2]
+
+    def column(row):
+        return jnp.sum(jnp.where(eye, row, 0.0), axis=1, keepdims=True)
+
+    def row(col):
+        return jnp.sum(jnp.where(eye, col, 0.0), axis=0, keepdims=True)
+
+    w0, w1 = column(rw[0:1, :]), column(rw[1:2, :])
+    e0, e1 = column(routes[0:1, :].astype(F32)), column(routes[1:2, :].astype(F32))
+    r0, r1 = e0.astype(jnp.int32), e1.astype(jnp.int32)
     h0, h1 = (lanes == r0), (lanes == r1)
     named = (h0.astype(F32) + h1.astype(F32)).astype(BF)
     before = (iota((128, 128), 0) > lanes).astype(BF)
     count = dot_nn(before, named)
-    t0 = r0.astype(F32) * CAP + jnp.sum(jnp.where(h0, count, 0.0), axis=1, keepdims=True)
-    t1 = r1.astype(F32) * CAP + jnp.sum(jnp.where(h1, count, 0.0), axis=1, keepdims=True)
-    u0 = jnp.sum(jnp.where(eye, t0, 0.0), axis=0, keepdims=True)
-    u1 = jnp.sum(jnp.where(eye, t1, 0.0), axis=0, keepdims=True)
+    t0 = e0 * CAP + jnp.sum(jnp.where(h0, count, 0.0), axis=1, keepdims=True)
+    t1 = e1 * CAP + jnp.sum(jnp.where(h1, count, 0.0), axis=1, keepdims=True)
+    u0, u1 = row(t0), row(t1)
     slots = iota((384, 128), 0).astype(F32)
     P0, P1 = (slots == u0).astype(BF), (slots == u1).astype(BF)
 
@@ -178,6 +186,10 @@
         def _(pos):
             tok(kind, pos, hc).start()
 
+    def send_token_pair(kind, p):
+        tok(kind, 2 * p, 0).start()
+        tok(kind, 2 * p + 1, 0).start()
+
     def keep(kind):
         src, dst = ((sx, rx), (sc, rc))[kind]
         dst[pl.ds(c * CAP, CAP)] = src[pl.ds(me_e * CAP, CAP)]
@@ -192,10 +204,6 @@
     keep(0)
     send_tokens(0, 1)
 
-    @on_core(0)
-    def _():
-        send_tokens(0, 0)
-
     @on_core(1)
     def _():
         relay(1, False)
@@ -204,8 +212,8 @@
     def _(m):
         k = pl.ds(pl.multiple_of(m * 256, 256), 256)
         cf = cot[:, k].astype(F32)
-        v0 = (cf * rw[:, 0:1]).astype(BF)
-        v1 = (cf * rw[:, 1:2]).astype(BF)
+        v0 = (cf * w0).astype(BF)
+        v1 = (cf * w1).astype(BF)
         UG[:, k] = (dot_nn(P0, v0) + dot_nn(P1, v1)).astype(BF)
     pack(UG, sc, 0, 10)
     keep(1)
@@ -213,28 +221,40 @@
 
     @on_core(0)
     def _():
+        pl.semaphore_wait(go, 1)
+        send_tokens(0, 0)
         send_tokens(1, 0)
 
     @on_core(1)
     def _():
-        @pl.loop(2, 7)
+        @pl.loop(2, 6)
         def _(t):
             relay(t, False)
+        pl.semaphore_signal(go, inc=1, device_id=(g, 2 * z))
+        relay(6, False)
         relay(7, True)
-        for way in range(2):
-            ring(way, 7, way).wait_recv()
-        W[g] = WZ[g]
-        for kind in range(2):
-            tok(kind, 0, 0).start()
-
-        @pl.loop(0, 12)
+        far = lax.rem(z + 8, 16)
+
+        @pl.loop(0, 6)
         def _(p):
             for i in range(15):
-                w_copy(1, i, p * 32, 32).start()
+                @pl.when(plane(PLANE[i]) != far)
+                def _():
+                    w_copy(1, i, p * 64, 64).start()
             for kind in range(2):
-                tok(kind, p + 1, 0).start()
+                send_token_pair(kind, p)
+        for way in range(2):
+            for h in range(3):
+                ring(way, 7, way * 3 + h).wait_recv()
+        for i in range(15):
+            @pl.when(plane(PLANE[i]) == far)
+            def _():
+                @pl.loop(0, 6)
+                def _(p):
+                    w_copy(1, i, p * 64, 64).start()
         for kind in range(2):
-            send_tokens(kind, 0, 13)
+            send_tokens(kind, 0, 12)
+        W[g] = WZ[g]
 
     for i in range(15):
         w_copy(0, i, 0, 384).wait_recv()
@@ -387,13 +407,13 @@
                 a0, a1 = carry
                 k = pl.ds(pl.multiple_of(m * 256, 256), 256)
                 o0, o1 = dot_nn(Q0, UO[:, k]), dot_nn(Q1, UO[:, k])
-                mixed[:, k] = (rw[:, 0:1] * o0 + rw[:, 1:2] * o1).astype(BF)
+                mixed[:, k] = (w0 * o0 + w1 * o1).astype(BF)
                 cf = cot[:, k].astype(F32)
                 return (a0 + jnp.sum(cf * o0, axis=1, keepdims=True),
                         a1 + jnp.sum(cf * o1, axis=1, keepdims=True))
             a0, a1 = lax.fori_loop(0, 8, body, (jnp.zeros((128, 1), F32), jnp.zeros((128, 1), F32)))
-            rgrad[:, 0:1] = a0
-            rgrad[:, 1:2] = a1
+            rgrad[0:1, :] = row(a0)
+            rgrad[1:2, :] = row(a1)
         else:
             UG[320:384, :] = jnp.zeros((64, 2048), BF)
             unpack(rg, UG, 0, 10)
@@ -472,9 +492,10 @@
         for way in range(2):
             @pl.loop(0, 7)
             def _(t):
-                for h in range(2):
+                for h in range(6):
                     ring(way, t, h).wait_send()
-            ring(way, 7, way).wait_send()
+            for h in range(3):
+                ring(way, 7, way * 3 + h).wait_send()
             for h in range(2):
                 hop(way, 0, h, True)[1].wait_send()
 
@@ -496,7 +517,7 @@
         out_shape=(
             jax.ShapeDtypeStruct((rows, width), BF),
             jax.ShapeDtypeStruct((rows, width), BF),
-            jax.ShapeDtypeStruct((rows, 2), F32),
+            jax.ShapeDtypeStruct((2, rows), F32),
             jax.ShapeDtypeStruct((ff, part), F32),
         ),
         in_specs=[pl.BlockSpec(memory_space=pltpu.VMEM)] * 7,
@@ -512,15 +533,16 @@
             pltpu.VMEM((16, 768, 128), BF), pltpu.VMEM((16, 768, 128), BF),
             pltpu.VMEM((2, 8, 768, 128), BF),
             flat(256, 256),
-            dma((15,)), dma((15,)), dma((2, 8, 2)), dma((2, 8, 2)),
+            dma((15,)), dma((15,)), dma((2, 8, 6)), dma((2, 8, 6)),
             dma((2, 32)), dma((2, 32)), dma((2, 32)), dma((2, 32)),
             dma((15,)), dma((16,)), dma((2, 8, 2)), dma((2, 8, 2)),
+            pltpu.SemaphoreType.REGULAR,
         ],
         compiler_params=pltpu.CompilerParams(
             collective_id=0, has_side_effects=True, vmem_limit_bytes=60 * 2**20),
-    )(routes, route_weight, tokens, cotangent, w_gate[0], w_up[0], w_down[0])
+    )(routes.T, route_weight.T, tokens, cotangent, w_gate[0], w_up[0], w_down[0])
     mixed, gtok, rgrad, gdown = out
-    return (mixed, gtok, rgrad, gdown[None])
+    return (mixed, gtok, rgrad.T, gdown[None])
 
 
 def solution(mesh):

time: 236 us -> 271 us (1.15)
  the two profiles are of different devices: /device:TPU:1 before, /device:TPU:19 now
where the time goes in v3:
time: 271 us
  Pallas kernels  266 us (98%)
  local copies, waits for them, and re-layouts  4.05 us (1%)
    pallas_call x1, Pallas kernels, shards(): pl.pallas_call(kernel, out_shape=(jax.ShapeDtypeStruct((rows, width), BF)...  266 us

profile of v3, /device:TPU:19, one launch (start us, length us, event | category | flops | bytes accessed | tf_op | source)
XLA Modules:
  0.0 271.0 jit_solution(14431042744008033587)
XLA Ops:
  0.6 266.3 %shard_map.102 = (bf16[128,2048]{1,0:T(8,128)(2,1)}, bf16[128,2048]{1,0:T(8,128)(2,1)}, f32[2,128]{1,0:T(2,128)}, f32[768,128]{1,0:T(8,128)}) custom-call(s32[2,128]{1,0:T(2,128)} %bitcast.11, f32[2,128]{1,0:T(2,128)} %bitcast.12, bf16[128,2048]{1,0:T(8,128)(2,1)} %x.1, bf16[128,2048]{1,0:T(8,128)(2,1)} %cot.1, bf16[128,768]{1,0:T(8,128)(2,1)} %bitcast.8, ...), custom_call_target="tpu_custom_call" | custom-call | tf_op jit(solution)/shard_map/pallas_call | solution.py:515
  266.9 0.0 copy-start
  266.9 1.9 copy.15
  268.9 0.0 copy-done
  268.9 0.0 copy-start.2
  268.9 0.0 copy-start.1
  268.9 0.8 copy.16
  269.7 0.0 copy-done.2
  269.7 0.6 copy.17
  270.2 0.0 copy-done.1
  270.2 0.7 copy.18
Async XLA Ops:
  266.9 2.0 copy-start
  268.9 0.8 copy-start.2
  268.9 1.4 copy-start.1

commit v4 on v2

--- a/solution.py
+++ b/solution.py
@@ -109,15 +109,23 @@
                 ring(way, 0, h).start()
 
     lanes = iota((128, 128), 1)
-    r0, r1 = routes[:, 0:1], routes[:, 1:2]
+
+    def column(row):
+        return jnp.sum(jnp.where(eye, row, 0.0), axis=1, keepdims=True)
+
+    def row(col):
+        return jnp.sum(jnp.where(eye, col, 0.0), axis=0, keepdims=True)
+
+    w0, w1 = column(rw[0:1, :]), column(rw[1:2, :])
+    e0, e1 = column(routes[0:1, :].astype(F32)), column(routes[1:2, :].astype(F32))
+    r0, r1 = e0.astype(jnp.int32), e1.astype(jnp.int32)
     h0, h1 = (lanes == r0), (lanes == r1)
     named = (h0.astype(F32) + h1.astype(F32)).astype(BF)
     before = (iota((128, 128), 0) > lanes).astype(BF)
     count = dot_nn(before, named)
-    t0 = r0.astype(F32) * CAP + jnp.sum(jnp.where(h0, count, 0.0), axis=1, keepdims=True)
-    t1 = r1.astype(F32) * CAP + jnp.sum(jnp.where(h1, count, 0.0), axis=1, keepdims=True)
-    u0 = jnp.sum(jnp.where(eye, t0, 0.0), axis=0, keepdims=True)
-    u1 = jnp.sum(jnp.where(eye, t1, 0.0), axis=0, keepdims=True)
+    t0 = e0 * CAP + jnp.sum(jnp.where(h0, count, 0.0), axis=1, keepdims=True)
+    t1 = e1 * CAP + jnp.sum(jnp.where(h1, count, 0.0), axis=1, keepdims=True)
+    u0, u1 = row(t0), row(t1)
     slots = iota((384, 128), 0).astype(F32)
     P0, P1 = (slots == u0).astype(BF), (slots == u1).astype(BF)
 
@@ -159,8 +167,8 @@
             e = 2 * j + 1
             dev = (j, 2 * z + 1)
         return pltpu.make_async_remote_copy(
-            src.at[pl.ds(e * CAP, CAP)], dst.at[pl.ds((2 * pos + c) * CAP, CAP)],
-            tss.at[kind, 2 * pos + hc], trs.at[kind, 2 * pos + c], device_id=dev)
+            src.at[pl.ds(e * CAP, CAP)], dst.at[pl.ds((16 * c + pos) * CAP, CAP)],
+            tss.at[kind, 16 * hc + pos], trs.at[kind, 16 * c + pos], device_id=dev)
 
     def tok_recv(kind, q):
         src, dst = ((sx, rx), (sc, rc))[kind]
@@ -180,7 +188,7 @@
 
     def keep(kind):
         src, dst = ((sx, rx), (sc, rc))[kind]
-        dst[pl.ds(c * CAP, CAP)] = src[pl.ds(me_e * CAP, CAP)]
+        dst[pl.ds(16 * c * CAP, CAP)] = src[pl.ds(me_e * CAP, CAP)]
 
     pa = (P0.astype(F32) + P1.astype(F32)).astype(BF)
 
@@ -204,8 +212,8 @@
     def _(m):
         k = pl.ds(pl.multiple_of(m * 256, 256), 256)
         cf = cot[:, k].astype(F32)
-        v0 = (cf * rw[:, 0:1]).astype(BF)
-        v1 = (cf * rw[:, 1:2]).astype(BF)
+        v0 = (cf * w0).astype(BF)
+        v1 = (cf * w1).astype(BF)
         UG[:, k] = (dot_nn(P0, v0) + dot_nn(P1, v1)).astype(BF)
     pack(UG, sc, 0, 10)
     keep(1)
@@ -244,8 +252,8 @@
         dev = (jnp.where(c == 0, g, chip(pos, -1)),
                jnp.where(c == 0, lax.rem(z + 16 - dz(pos), 16), z) * 2 + cc)
         return pltpu.make_async_remote_copy(
-            src.at[pl.ds((2 * pos + cc) * CAP, CAP)], dst.at[pl.ds(me_e * CAP, CAP)],
-            bss.at[kind, 2 * pos + cc], brs.at[kind, me_e], device_id=dev)
+            src.at[pl.ds((16 * cc + pos) * CAP, CAP)], dst.at[pl.ds(me_e * CAP, CAP)],
+            bss.at[kind, 16 * cc + pos], brs.at[kind, me_e], device_id=dev)
 
     def back_recv(kind, e):
         src, dst = ((po, ro), (pg, rg))[kind]
@@ -253,12 +261,9 @@
             src.at[pl.ds(0, CAP)], dst.at[pl.ds(e * CAP, CAP)],
             bss.at[kind, e], brs.at[kind, e], device_id=(g, s + 1 - 2 * c))
 
-    def phase_a(half):
+    def phase_a(half, own):
         for kind in range(2):
-            if half == 0:
-                tok_recv(kind, 1 - c).wait_recv()
-
-            @pl.loop(half * 16 + (2 if half == 0 else 0), half * 16 + 16)
+            @pl.loop(half * 16 + (1 if half == own else 0), half * 16 + 16)
             def _(q):
                 tok_recv(kind, q).wait_recv()
         lo = half * 160
@@ -279,7 +284,7 @@
             GG[rows, k] = (gh * up * sig * (1.0 + gate * (1.0 - sig))).astype(BF)
             GU[rows, k] = (gh * act).astype(BF)
 
-    def phase_b(half):
+    def phase_b(half, own):
         lo = half * 160
         rows = pl.ds(lo, 160)
 
@@ -293,14 +298,12 @@
         for kind in range(2):
             src, dst, flat = ((po, ro, OO), (pg, rg, GP))[kind]
             pack(flat, src, lo, 5)
-            if half == 0:
-                back(kind, 0, 1 - c).start()
-                dst[pl.ds(me_e * CAP, CAP)] = src[pl.ds(c * CAP, CAP)]
-
-            @pl.loop(half * 8 + (1 if half == 0 else 0), half * 8 + 8)
+            if half == own:
+                dst[pl.ds(me_e * CAP, CAP)] = src[pl.ds(16 * own * CAP, CAP)]
+
+            @pl.loop(1 if half == own else 0, 16)
             def _(pos):
-                back(kind, pos, 0).start()
-                back(kind, pos, 1).start()
+                back(kind, pos, half).start()
 
     def g_copy(i, r, n):
         p = plane(PLANE[i])
@@ -387,13 +390,13 @@
                 a0, a1 = carry
                 k = pl.ds(pl.multiple_of(m * 256, 256), 256)
                 o0, o1 = dot_nn(Q0, UO[:, k]), dot_nn(Q1, UO[:, k])
-                mixed[:, k] = (rw[:, 0:1] * o0 + rw[:, 1:2] * o1).astype(BF)
+                mixed[:, k] = (w0 * o0 + w1 * o1).astype(BF)
                 cf = cot[:, k].astype(F32)
                 return (a0 + jnp.sum(cf * o0, axis=1, keepdims=True),
                         a1 + jnp.sum(cf * o1, axis=1, keepdims=True))
             a0, a1 = lax.fori_loop(0, 8, body, (jnp.zeros((128, 1), F32), jnp.zeros((128, 1), F32)))
-            rgrad[:, 0:1] = a0
-            rgrad[:, 1:2] = a1
+            rgrad[0:1, :] = row(a0)
+            rgrad[1:2, :] = row(a1)
         else:
             UG[320:384, :] = jnp.zeros((64, 2048), BF)
             unpack(rg, UG, 0, 10)
@@ -406,20 +409,24 @@
     @on_core(0)
     def _():
         for half in range(2):
-            phase_a(half)
-            phase_b(half)
+            phase_a(half, 0)
+            phase_b(half, 0)
         gradients()
 
     @on_core(1)
     def _():
-        phase_a(0)
-        phase_a(1)
+        phase_a(0, 1)
+        phase_a(1, 1)
         gradients()
-        phase_b(0)
-        phase_b(1)
+        phase_b(0, 1)
+        phase_b(1, 1)
+
+    combine(0)
+
+    @on_core(1)
+    def _():
         reduce_z()
 
-    combine(0)
     combine(1)
 
     @on_core(0)
@@ -496,7 +503,7 @@
         out_shape=(
             jax.ShapeDtypeStruct((rows, width), BF),
             jax.ShapeDtypeStruct((rows, width), BF),
-            jax.ShapeDtypeStruct((rows, 2), F32),
+            jax.ShapeDtypeStruct((2, rows), F32),
             jax.ShapeDtypeStruct((ff, part), F32),
         ),
         in_specs=[pl.BlockSpec(memory_space=pltpu.VMEM)] * 7,
@@ -518,9 +525,9 @@
         ],
         compiler_params=pltpu.CompilerParams(
             collective_id=0, has_side_effects=True, vmem_limit_bytes=60 * 2**20),
-    )(routes, route_weight, tokens, cotangent, w_gate[0], w_up[0], w_down[0])
+    )(routes.T, route_weight.T, tokens, cotangent, w_gate[0], w_up[0], w_down[0])
     mixed, gtok, rgrad, gdown = out
-    return (mixed, gtok, rgrad, gdown[None])
+    return (mixed, gtok, rgrad.T, gdown[None])
 
 
 def solution(mesh):

time: 236 us -> 263 us (1.11)
  Pallas kernels: 228 us -> 258 us
  local copies, waits for them, and re-layouts: 7.5 us -> 4.05 us
    pallas_call x1, Pallas kernels: 228 us -> 258 us  [shards(): pl.pallas_call(kernel, out_shape=(jax.ShapeDtypeStruct((rows, width), BF)...]
    unnamed x14 -> x10, local copies, waits for them, and re-layouts: 7.5 us -> 4.05 us
where the time goes in v4:
time: 263 us
  Pallas kernels  258 us (98%)
  local copies, waits for them, and re-layouts  4.05 us (2%)
    pallas_call x1, Pallas kernels, shards(): pl.pallas_call(kernel, out_shape=(jax.ShapeDtypeStruct((rows, width), BF)...  258 us

profile of v4, /device:TPU:1, one launch (start us, length us, event | category | flops | bytes accessed | tf_op | source)
XLA Modules:
  0.0 262.6 jit_solution(13804572780610112875)
XLA Ops:
  0.6 257.9 %shard_map.102 = (bf16[128,2048]{1,0:T(8,128)(2,1)}, bf16[128,2048]{1,0:T(8,128)(2,1)}, f32[2,128]{1,0:T(2,128)}, f32[768,128]{1,0:T(8,128)}) custom-call(s32[2,128]{1,0:T(2,128)} %bitcast.11, f32[2,128]{1,0:T(2,128)} %bitcast.12, bf16[128,2048]{1,0:T(8,128)(2,1)} %x.1, bf16[128,2048]{1,0:T(8,128)(2,1)} %cot.1, bf16[128,768]{1,0:T(8,128)(2,1)} %bitcast.8, ...), custom_call_target="tpu_custom_call" | custom-call | tf_op jit(solution)/shard_map/pallas_call | solution.py:501
  258.5 0.0 copy-start
  258.5 1.9 copy.15
  260.5 0.0 copy-done
  260.5 0.0 copy-start.2
  260.5 0.0 copy-start.1
  260.5 0.8 copy.16
  261.3 0.0 copy-done.2
  261.3 0.6 copy.17
  261.8 0.0 copy-done.1
  261.8 0.7 copy.18
Async XLA Ops:
  258.5 2.0 copy-start
  260.5 0.8 copy-start.2
  260.5 1.4 copy-start.1

commit v5 on v2

--- a/solution.py
+++ b/solution.py
@@ -109,15 +109,23 @@
                 ring(way, 0, h).start()
 
     lanes = iota((128, 128), 1)
-    r0, r1 = routes[:, 0:1], routes[:, 1:2]
+
+    def column(row):
+        return jnp.sum(jnp.where(eye, row, 0.0), axis=1, keepdims=True)
+
+    def row(col):
+        return jnp.sum(jnp.where(eye, col, 0.0), axis=0, keepdims=True)
+
+    w0, w1 = column(rw[0:1, :]), column(rw[1:2, :])
+    e0, e1 = column(routes[0:1, :].astype(F32)), column(routes[1:2, :].astype(F32))
+    r0, r1 = e0.astype(jnp.int32), e1.astype(jnp.int32)
     h0, h1 = (lanes == r0), (lanes == r1)
     named = (h0.astype(F32) + h1.astype(F32)).astype(BF)
     before = (iota((128, 128), 0) > lanes).astype(BF)
     count = dot_nn(before, named)
-    t0 = r0.astype(F32) * CAP + jnp.sum(jnp.where(h0, count, 0.0), axis=1, keepdims=True)
-    t1 = r1.astype(F32) * CAP + jnp.sum(jnp.where(h1, count, 0.0), axis=1, keepdims=True)
-    u0 = jnp.sum(jnp.where(eye, t0, 0.0), axis=0, keepdims=True)
-    u1 = jnp.sum(jnp.where(eye, t1, 0.0), axis=0, keepdims=True)
+    t0 = e0 * CAP + jnp.sum(jnp.where(h0, count, 0.0), axis=1, keepdims=True)
+    t1 = e1 * CAP + jnp.sum(jnp.where(h1, count, 0.0), axis=1, keepdims=True)
+    u0, u1 = row(t0), row(t1)
     slots = iota((384, 128), 0).astype(F32)
     P0, P1 = (slots == u0).astype(BF), (slots == u1).astype(BF)
 
@@ -204,8 +212,8 @@
     def _(m):
         k = pl.ds(pl.multiple_of(m * 256, 256), 256)
         cf = cot[:, k].astype(F32)
-        v0 = (cf * rw[:, 0:1]).astype(BF)
-        v1 = (cf * rw[:, 1:2]).astype(BF)
+        v0 = (cf * w0).astype(BF)
+        v1 = (cf * w1).astype(BF)
         UG[:, k] = (dot_nn(P0, v0) + dot_nn(P1, v1)).astype(BF)
     pack(UG, sc, 0, 10)
     keep(1)
@@ -387,13 +395,13 @@
                 a0, a1 = carry
                 k = pl.ds(pl.multiple_of(m * 256, 256), 256)
                 o0, o1 = dot_nn(Q0, UO[:, k]), dot_nn(Q1, UO[:, k])
-                mixed[:, k] = (rw[:, 0:1] * o0 + rw[:, 1:2] * o1).astype(BF)
+                mixed[:, k] = (w0 * o0 + w1 * o1).astype(BF)
                 cf = cot[:, k].astype(F32)
                 return (a0 + jnp.sum(cf * o0, axis=1, keepdims=True),
                         a1 + jnp.sum(cf * o1, axis=1, keepdims=True))
             a0, a1 = lax.fori_loop(0, 8, body, (jnp.zeros((128, 1), F32), jnp.zeros((128, 1), F32)))
-            rgrad[:, 0:1] = a0
-            rgrad[:, 1:2] = a1
+            rgrad[0:1, :] = row(a0)
+            rgrad[1:2, :] = row(a1)
         else:
             UG[320:384, :] = jnp.zeros((64, 2048), BF)
             unpack(rg, UG, 0, 10)
@@ -496,7 +504,7 @@
         out_shape=(
             jax.ShapeDtypeStruct((rows, width), BF),
             jax.ShapeDtypeStruct((rows, width), BF),
-            jax.ShapeDtypeStruct((rows, 2), F32),
+            jax.ShapeDtypeStruct((2, rows), F32),
             jax.ShapeDtypeStruct((ff, part), F32),
         ),
         in_specs=[pl.BlockSpec(memory_space=pltpu.VMEM)] * 7,
@@ -518,9 +526,9 @@
         ],
         compiler_params=pltpu.CompilerParams(
             collective_id=0, has_side_effects=True, vmem_limit_bytes=60 * 2**20),
-    )(routes, route_weight, tokens, cotangent, w_gate[0], w_up[0], w_down[0])
+    )(routes.T, route_weight.T, tokens, cotangent, w_gate[0], w_up[0], w_down[0])
     mixed, gtok, rgrad, gdown = out
-    return (mixed, gtok, rgrad, gdown[None])
+    return (mixed, gtok, rgrad.T, gdown[None])
 
 
 def solution(mesh):

time: 236 us -> 232 us (0.983)
  local copies, waits for them, and re-layouts: 7.5 us -> 4.05 us
    unnamed x14 -> x10, local copies, waits for them, and re-layouts: 7.5 us -> 4.05 us
where the time goes in v5:
time: 232 us
  Pallas kernels  228 us (98%)
  local copies, waits for them, and re-layouts  4.05 us (2%)
    pallas_call x1, Pallas kernels, shards(): pl.pallas_call(kernel, out_shape=(jax.ShapeDtypeStruct((rows, width), BF)...  228 us

profile of v5, /device:TPU:1, one launch (start us, length us, event | category | flops | bytes accessed | tf_op | source)
XLA Modules:
  0.0 232.3 jit_solution(1924619838462229277)
XLA Ops:
  0.6 227.6 %shard_map.102 = (bf16[128,2048]{1,0:T(8,128)(2,1)}, bf16[128,2048]{1,0:T(8,128)(2,1)}, f32[2,128]{1,0:T(2,128)}, f32[768,128]{1,0:T(8,128)}) custom-call(s32[2,128]{1,0:T(2,128)} %bitcast.11, f32[2,128]{1,0:T(2,128)} %bitcast.12, bf16[128,2048]{1,0:T(8,128)(2,1)} %x.1, bf16[128,2048]{1,0:T(8,128)(2,1)} %cot.1, bf16[128,768]{1,0:T(8,128)(2,1)} %bitcast.8, ...), custom_call_target="tpu_custom_call" | custom-call | tf_op jit(solution)/shard_map/pallas_call | solution.py:502
  228.2 0.0 copy-start
  228.2 1.9 copy.15
  230.2 0.0 copy-done
  230.2 0.0 copy-start.2
  230.2 0.0 copy-start.1
  230.2 0.8 copy.16
  231.0 0.0 copy-done.2
  231.0 0.6 copy.17
  231.5 0.0 copy-done.1
  231.5 0.7 copy.18
Async XLA Ops:
  228.2 2.0 copy-start
  230.2 0.8 copy-start.2
  230.2 1.4 copy-start.1

commit v6 on v5

--- a/solution.py
+++ b/solution.py
@@ -338,7 +338,7 @@
     def hop(way, t, h, first=False):
         to = up_z(1 - 2 * way)
         j = lax.rem(z + 16 + (t - 7 if way else 8 - t), 16)
-        r = pl.ds(h * 384, 384)
+        r = pl.ds(h * 192, 192)
         src = GR.at[j, r] if first else RS.at[way, t - 1, r]
         return j, pltpu.make_async_remote_copy(
             src, RS.at[way, t, r], rss.at[way, t, h], rrs.at[way, t, h], device_id=(g, 2 * to + 1))
@@ -350,23 +350,23 @@
 
     def reduce_z():
         for way in range(2):
-            for h in range(2):
+            for h in range(4):
                 j, cp = hop(way, 0, h, True)
                 if h == 0:
                     g_wait(j)
                 cp.start()
 
         def step(t, ways):
-            for h in range(2):
+            for h in range(4):
                 for way in ways:
                     j, cp = hop(way, t, h)
                     if h == 0:
                         g_wait(j)
                     hop(way, t - 1, h, True)[1].wait_recv()
 
-                    @pl.loop(0, 6)
+                    @pl.loop(0, 3)
                     def _(b):
-                        r = pl.ds(pl.multiple_of(h * 384 + b * 64, 64), 64)
+                        r = pl.ds(pl.multiple_of(h * 192 + b * 64, 64), 64)
                         RS[way, t - 1, r, :] = (RS[way, t - 1, r, :].astype(F32)
                                                 + GR[j, r, :].astype(F32)).astype(BF)
                     cp.start()
@@ -446,7 +446,7 @@
 
     @on_core(1)
     def _():
-        for h in range(2):
+        for h in range(4):
             hop(0, 7, h, True)[1].wait_recv()
             hop(1, 6, h, True)[1].wait_recv()
 
@@ -483,12 +483,12 @@
                 for h in range(2):
                     ring(way, t, h).wait_send()
             ring(way, 7, way).wait_send()
-            for h in range(2):
+            for h in range(4):
                 hop(way, 0, h, True)[1].wait_send()
 
             @pl.loop(1, 8 - way)
             def _(t):
-                for h in range(2):
+                for h in range(4):
                     hop(way, t, h, True)[1].wait_send()
 
 
@@ -522,7 +522,7 @@
             flat(256, 256),
             dma((15,)), dma((15,)), dma((2, 8, 2)), dma((2, 8, 2)),
             dma((2, 32)), dma((2, 32)), dma((2, 32)), dma((2, 32)),
-            dma((15,)), dma((16,)), dma((2, 8, 2)), dma((2, 8, 2)),
+            dma((15,)), dma((16,)), dma((2, 8, 4)), dma((2, 8, 4)),
         ],
         compiler_params=pltpu.CompilerParams(
             collective_id=0, has_side_effects=True, vmem_limit_bytes=60 * 2**20),

time: 232 us -> 231 us (level)
  Pallas kernels: 228 us -> 225 us
where the time goes in v6:
time: 231 us; the launch traced here: 230 us
  Pallas kernels  225 us (97%)
  local copies, waits for them, and re-layouts  4.05 us (2%)
    pallas_call x1, Pallas kernels, shards(): pl.pallas_call(kernel, out_shape=(jax.ShapeDtypeStruct((rows, width), BF)...  225 us

profile of v6, /device:TPU:1, one launch (start us, length us, event | category | flops | bytes accessed | tf_op | source)
XLA Modules:
  0.0 230.1 jit_solution(7523967662183034662)
XLA Ops:
  0.6 225.4 %shard_map.102 = (bf16[128,2048]{1,0:T(8,128)(2,1)}, bf16[128,2048]{1,0:T(8,128)(2,1)}, f32[2,128]{1,0:T(2,128)}, f32[768,128]{1,0:T(8,128)}) custom-call(s32[2,128]{1,0:T(2,128)} %bitcast.11, f32[2,128]{1,0:T(2,128)} %bitcast.12, bf16[128,2048]{1,0:T(8,128)(2,1)} %x.1, bf16[128,2048]{1,0:T(8,128)(2,1)} %cot.1, bf16[128,768]{1,0:T(8,128)(2,1)} %bitcast.8, ...), custom_call_target="tpu_custom_call" | custom-call | tf_op jit(solution)/shard_map/pallas_call | solution.py:502
  226.0 0.0 copy-start
  226.0 1.9 copy.15
  228.0 0.0 copy-done
  228.0 0.0 copy-start.2
  228.0 0.0 copy-start.1
  228.0 0.8 copy.16
  228.8 0.0 copy-done.2
  228.8 0.6 copy.17
  229.3 0.0 copy-done.1
  229.3 0.7 copy.18
Async XLA Ops:
  226.0 2.0 copy-start
  228.0 0.8 copy-start.2
  228.0 1.4 copy-start.1
